TPU v7x, 768 devices: a whole 4x8x12 slice. The times are simulated.
768 devices in a mesh: dp: 96 (over x, z, core), owner: 8 (over y).
Axes of the slice: x: 4, y: 8, z: 12, core: 2. Of those that a mesh axis runs over, the one named last changes fastest.
Arguments:
- grad_parts: bfloat16 [96, 192, 256, 256], P('dp', None, 'owner'), may hold values from -3 to 3
- stats_in: float32 [96, 16, 256, 256], P('dp', 'owner'), may hold values from -16 to 8192, as said below
- assignment: int32 [96, 4, 1], P('dp'), may hold values from 0 to 7; in each aligned block of 4 rows (0 to 3, 4 to 7, ..., all dimensions but the last counted through in order) at most 2 rows name the same one
Outputs:
- update: bfloat16 [192, 256, 256], P('dp', 'owner')
- stats_out: float32 [96, 16, 256, 256], P('dp', 'owner')
Inputs may be any that keep to these rules, and one draw needn't show every extreme that they name: `assignment`: in each dp index's 4 tasks no owner index is named more than 2 times. Every 256 x 256 matrix of stats_in is symmetric positive definite.
All inputs are finite; a program needn't handle non-finite values.
Results may differ from a plain program's by a relative error of at most 0.0069.
Values may be sent and summed in bfloat16 or wider, within the bound.
A program may use at most 32 MiB of HBM per device.

v0:
```python
import jax
import jax.numpy as jnp
from jax import lax
from jax.sharding import PartitionSpec as P

CAP = 2


DECAY_RATE = 0.95
NORM_EPSILON = 1e-06


def matmul_high(left_side, right_side):
    return jnp.matmul(left_side, right_side, precision=lax.Precision.HIGHEST)


def slot_table(owner_list):
    positions = jnp.arange(owner_list.shape[0], dtype=jnp.int32)
    same_owner = owner_list[:, None] == owner_list[None, :]
    earlier = positions[None, :] < positions[:, None]
    slot_rank = jnp.sum(jnp.logical_and(same_owner, earlier).astype(jnp.int32), axis=1)
    return (owner_list * CAP + slot_rank, slot_rank)


def inverse_root(stats_all):
    identity = jnp.eye(stats_all.shape[-1], dtype=jnp.float32)
    norm_value = jnp.sqrt(jnp.sum(stats_all * stats_all, axis=(1, 2), keepdims=True) + NORM_EPSILON)
    matrix = stats_all / norm_value
    factor = (5.0 * identity - matrix) * 0.25
    current = factor
    square = matmul_high(factor, factor)
    matrix = matmul_high(matmul_high(square, square), matrix)
    factor = (5.0 * identity - matrix) * 0.25
    current = matmul_high(current, factor)
    return current.astype(jnp.bfloat16)


def per_device(grad_parts, stats_in, assignment):
    partial_rows = grad_parts[0]
    summed = lax.psum_scatter(
        partial_rows.astype(jnp.float32), "dp", scatter_dimension=0, tiled=True
    )
    own_rows = summed.astype(jnp.bfloat16)
    slab_rows = own_rows.shape[1]
    blocks = lax.all_gather(own_rows, "owner", axis=1, tiled=True)
    block_count = blocks.shape[0]
    owner_list = assignment[0, :, 0]
    task_count = owner_list.shape[0]
    slots, slot_rank = slot_table(owner_list)
    owner_here = lax.axis_index("owner")
    local_ids = owner_here * CAP + jnp.arange(CAP, dtype=jnp.int32)
    matches = (slots[None, :] == local_ids[:, None]).astype(jnp.int32)
    in_use = jnp.sum(matches, axis=1) > 0
    task_ids = jnp.arange(task_count, dtype=jnp.int32)
    block_pick = (
        task_ids[:, None] // 2 == jnp.arange(block_count, dtype=jnp.int32)[None, :]
    ).astype(jnp.int32)
    chosen = jnp.dot(matches, block_pick)
    side_flag = jnp.sum(matches * (task_ids % 2)[None, :], axis=1)
    selected = jnp.einsum(
        "cj,jab->cab", chosen.astype(jnp.bfloat16), blocks, preferred_element_type=jnp.float32
    ).astype(jnp.bfloat16)
    oriented = jnp.where(side_flag[:, None, None] == 1, jnp.swapaxes(selected, 1, 2), selected)
    gram_matrix = jnp.einsum("cik,cjk->cij", oriented, oriented, preferred_element_type=jnp.float32)
    stats_new = jnp.where(in_use[:, None, None], DECAY_RATE * stats_in[0] + gram_matrix, 0.0)
    roots = inverse_root(stats_new)
    all_roots = lax.all_gather(roots, "owner", axis=0, tiled=True)
    task_roots = jnp.take(all_roots, slots, axis=0)
    left_roots = task_roots[0::2]
    right_roots = task_roots[1::2]
    blocks_wide = blocks.astype(jnp.float32)
    grad_squares = jnp.sum(blocks_wide * blocks_wide, axis=(1, 2))
    row_start = owner_here * slab_rows
    half_product = jnp.einsum(
        "jik,jkl->jil", left_roots, blocks, preferred_element_type=jnp.float32
    ).astype(jnp.bfloat16)
    preconditioned = jnp.einsum(
        "jik,jkl->jil", half_product, right_roots, preferred_element_type=jnp.float32
    )
    pre_squares = jnp.sum(preconditioned * preconditioned, axis=(1, 2))
    pre_rows = lax.dynamic_slice_in_dim(preconditioned, row_start, slab_rows, 1)
    graft_scale = jnp.sqrt(grad_squares + NORM_EPSILON) / jnp.sqrt(pre_squares + NORM_EPSILON)
    update = (pre_rows * graft_scale[:, None, None]).astype(jnp.bfloat16)
    return (update, stats_new[None])


def solution(mesh):
    in_specs = (P("dp", None, "owner", None), P("dp", "owner", None, None), P("dp", None, None))
    out_specs = (P("dp", "owner", None), P("dp", "owner", None, None))
    return jax.shard_map(
        per_device, mesh=mesh, in_specs=in_specs, out_specs=out_specs, check_vma=False
    )
```

profile of v0, /device:TPU:2, one launch (start us, length us, event | category | flops | bytes accessed | tf_op | source)
XLA Modules:
  0.0 322.9 jit_solution(1407230016351409880)
XLA Ops:
  7.2 0.0 reduce-scatter.2.cloned.1.call-start
  7.2 5.3 %bitcast_convert_fusion = f32[192,32,256]{2,1,0:T(8,128)} fusion(bf16[1,192,32,256]{3,2,1,0:T(8,128)(2,1)} %param.3), kind=kLoop, calls=%fused_computation.1 | loop fusion | flops 1572864 | bytes 9437184 | tf_op jit(solution)/shard_map/convert_element_type | solution.py:41
  12.5 0.0 copy-start.2
  12.5 0.0 copy-start
  12.5 0.0 reduce-scatter.2.cloned.1.call-update
  12.6 0.0 all-gather.2.cloned.1.call-start
  12.6 0.5 copy-done.2
  13.2 0.2 convert_reduce_fusion
  13.4 0.2 fusion.18
  13.6 223.1 %reduce-scatter.2.cloned.1.call-done = f32[2,32,256]{2,1,0:T(8,128)} async-done(((f32[192,32,256]{2,1,0:T(8,128)}), f32[2,32,256]{2,1,0:T(8,128)}) %reduce-scatter.2.cloned.1.call-update) | async-done | bytes 65552 | tf_op jit(solution)/shard_map/reduce_scatter | solution.py:40
  236.7 0.8 convert_element_type.41
  237.6 25.8 %all_gather.6 = bf16[2,256,256]{2,0,1:T(2,128)(2,1)S(1)} all-gather(bf16[2,32,256]{2,0,1:T(2,128)(2,1)S(1)} %copy.13), channel_id=1, replica_groups=mesh['dp'=96,'owner'=8] {'owner'}, dimensions={1}, use_global_device_ids=true | all-gather | bytes 294912 | tf_op jit(solution)/shard_map/all_gather | solution.py:45
  263.4 0.6 convolution_convert_fusion.2
  264.0 0.5 copy.14
  264.5 0.4 broadcast_select_fusion
  264.9 0.0 copy-done
  264.9 0.4 multiply_reduce_fusion.2
  265.3 0.0 copy-start.1
  265.3 0.8 fusion.3
  266.1 0.7 fusion.33
  266.8 0.7 fusion
  267.5 1.4 convolution_convert_fusion.1
  269.0 0.0 copy-done.1
  269.0 0.0 all-gather.2.cloned.1.call-update
  269.0 0.7 multiply_reduce_fusion.1
  269.7 42.9 %all-gather.2.cloned.1.call-done = bf16[16,256,256]{2,1,0:T(8,128)(2,1)} async-done(((bf16[2,256,256]{2,1,0:T(8,128)(2,1)}), bf16[16,256,256]{2,1,0:T(8,128)(2,1)}) %all-gather.2.cloned.1.call-update) | async-done | bytes 2097168 | tf_op jit(solution)/shard_map/all_gather | solution.py:67
  312.6 2.2 gather_fusion
  314.8 0.1 broadcast_select_fusion.1
  314.9 0.5 multiply_reduce_fusion
  315.4 0.7 multiply_convert_fusion
  (11 shorter events, 0.1 us)
Async XLA Ops:
  7.2 229.6 %reduce-scatter.2.cloned.1.call-start = ((), (), s32[]{:S(2)}) async-start(), calls=%async_computation.1 | async-start | bytes 6356992 | tf_op jit(solution)/shard_map/reduce_scatter | solution.py:40
  12.5 0.7 copy-start.2
  12.5 252.4 %copy-start = (f32[1,2,256,256]{3,2,1,0:T(8,128)S(1)}, f32[1,2,256,256]{3,2,1,0:T(8,128)}, u32[]{:S(2)}) copy-start(f32[1,2,256,256]{3,2,1,0:T(8,128)} %param.4) | copy-start | bytes 1572868
  12.6 300.1 %all-gather.2.cloned.1.call-start = ((), (), s32[]{:S(2)}) async-start(), calls=%async_computation.2 | async-start | bytes 2359296 | tf_op jit(solution)/shard_map/all_gather | solution.py:67
  265.3 3.7 %copy-start.1 = (f32[2,256,256]{2,1,0:T(8,128)}, f32[2,256,256]{2,1,0:T(8,128)S(1)}, u32[]{:S(2)}) copy-start(f32[2,256,256]{2,1,0:T(8,128)S(1)} %get-tuple-element.7) | copy-start | bytes 1572868
Sparse Core Ops, SparseCore 0:
  13.3 223.3 reduce-scatter.1
  269.1 43.4 all-gather.1
where the time goes:
time: 323 us
  waiting for transfers between devices  266 us (82%)
  blocking collectives  25.8 us (8%)
  between operations  14.2 us (4%)
  other arithmetic  8.44 us (3%)
  matrix products  5.1 us (2%)
  local copies, waits for them, and re-layouts  3.27 us (1%)
    reduce_scatter x1, waiting for transfers between devices, per_device(): lax.psum_scatter(partial_rows.astype(jnp.float32), 'dp', scatter_dimensio...  223 us
    all_gather x1, waiting for transfers between devices, per_device(): all_roots = lax.all_gather(roots, 'owner', axis=0, tiled=True)  42.9 us
    all_gather x1, blocking collectives, per_device(): blocks = lax.all_gather(own_rows, 'owner', axis=1, tiled=True)  25.8 us
  transfers between devices with their start and end apart: 2, of which 2 were waited for; matrix products, arithmetic and copies ran while one was open for 0% of the time, Pallas kernels for 0%

commit v1 on v0

v1 whole, which is shorter than its diff:
```python
import functools

import jax
import jax.numpy as jnp
from jax import lax
from jax.experimental import pallas as pl
from jax.experimental.pallas import tpu as pltpu
from jax.sharding import PartitionSpec as P

NX, NZ, NC, NY = 4, 12, 2, 8
BLOCKS = 2
TASKS = 4
CAP = 2
BS = 256
ROWS = BS // NY
HALF = ROWS // 2
FAR = 5
DECAY_RATE = 0.95
NORM_EPSILON = 1e-06
MESH = pl.DeviceIdType.MESH
F32 = jnp.float32
BF16 = jnp.bfloat16

Z_ORDER = [(6 + (1 - 2 * (q % 2)) * ((q + 1) // 2)) % NZ for q in range(NZ)]

CORE = 0
X_OPP = CORE + NX * BLOCKS
X_A = X_OPP + 2 * BLOCKS
X_BF = X_A + 2 * BLOCKS
X_BN = X_BF + 2 * BLOCKS
Z_FAR = X_BN + 2 * BLOCKS
Z_NEAR = Z_FAR + 6 * BLOCKS
Y_SLOT = Z_NEAR + 6 * BLOCKS
Y_TASK = Y_SLOT + NY
Y_GRAD = Y_TASK + NY
N_SEMS = Y_GRAD + NY * BLOCKS
L_OWN = 0
L_STATS = L_OWN + NX * BLOCKS
L_OUT = L_STATS + 1
N_LOCAL = L_OUT + 2


def dot(left, right, dims=((1,), (0,))):
    return lax.dot_general(left, right, (dims, ((), ())), preferred_element_type=F32)


def inverse_root(stats):
    scale = 0.25 * lax.rsqrt(jnp.sum(stats * stats) + NORM_EPSILON)
    quarter = stats * scale
    quarter16 = quarter.astype(BF16)
    excess = dot(quarter16, quarter16) - 2.5 * quarter
    excess16 = excess.astype(BF16)
    fourth = (3.125 * excess + dot(excess16, excess16)).astype(BF16)
    carried = 2.44140625 * quarter + dot(fourth, quarter16)
    rows = lax.broadcasted_iota(jnp.int32, (BS, BS), 0)
    columns = lax.broadcasted_iota(jnp.int32, (BS, BS), 1)
    diagonal = jnp.where(rows == columns, F32(1.5625), F32(0.0))
    root = diagonal - 1.25 * (quarter + carried) + dot(quarter16, carried.astype(BF16))
    return root.astype(BF16)


def kernel(parts, stats_in, assign, update, stats_out,
           own, other, chip, rx_opp, rx_a, rx_b, tx_b, xs, xs_own, rz6, rz54, tx_z, rz_near,
           grad, slots_in, slots16, slot_rows, task_stats, gram, new_stats, pre_ref, upd_rows,
           send_sems, recv_sems, local_sems):
    dp = lax.axis_index("dp")
    y = lax.axis_index("owner")
    x, z, core = dp // (NZ * NC), (dp // NC) % NZ, dp % NC

    def device(dx=0, dz=0, dc=0, dy=0):
        return (
            (((x + dx + NX) % NX) * NZ + (z + dz + NZ) % NZ) * NC + (core + dc) % NC,
            (y + dy + NY) % NY,
        )

    sent = []

    def send(src, dst, number, target):
        copy = pltpu.make_async_remote_copy(
            src_ref=src, dst_ref=dst, send_sem=send_sems.at[number], recv_sem=recv_sems.at[number],
            device_id=target, device_id_type=MESH,
        )
        copy.start()
        sent.append(copy)
        return copy

    own_loads = {}
    for j in range(BLOCKS):
        for k in (2, 1, 3, 0):
            copy = pltpu.make_async_copy(
                parts.at[(x + k) % NX, :, core, j], own.at[k, j], local_sems.at[L_OWN + k * BLOCKS + j]
            )
            own_loads[k, j] = copy
    stats_load = pltpu.make_async_copy(stats_in, slots_in, local_sems.at[L_STATS])

    partners = [device(dc=1), device(dx=1), device(dx=-1)]
    partners += [device(dz=d) for d in (1, 2, 3, -1, -2, -3)]
    partners += [device(dy=d) for d in range(1, NY)]
    barrier = pltpu.get_barrier_semaphore()
    for partner in partners:
        pl.semaphore_signal(barrier, inc=1, device_id=partner, device_id_type=MESH)
    stats_load.start()
    for copy in own_loads.values():
        copy.start()
    stats_load.wait()
    slots16[...] = slots_in[...].astype(BF16)
    pl.semaphore_wait(barrier, len(partners))

    core_copies = {}
    for j in range(BLOCKS):
        for k in (2, 1, 3, 0):
            core_copies[k, j] = send(
                parts.at[(x + k) % NX, :, 1 - core, j], other.at[k, j], CORE + k * BLOCKS + j, device(dc=1)
            )

    my_rows = pl.ds(pl.multiple_of(y * ROWS, ROWS), ROWS)
    slot_copies = []
    for d in (4, 3, 5, 2, 6, 1, 7):
        target_rows = pl.ds(pl.multiple_of(((y + d) % NY) * ROWS, ROWS), ROWS)
        slot_copies.append(
            send(slots16.at[:, target_rows], slot_rows.at[y], Y_SLOT + d, device(dy=d))
        )
    slot_rows[y] = slots16[:, my_rows]

    def chip_sum(k, j):
        own_loads[k, j].wait()
        core_copies[k, j].wait_recv()

        def step(q, carry):
            place = (z + 6 + (1 - 2 * (q % 2)) * ((q + 1) // 2)) % NZ
            total = own[k, j, place].astype(F32) + other[k, j, place].astype(F32)
            chip[k, j, q] = total.astype(BF16)
            return carry

        lax.fori_loop(0, NZ, step, 0)

    low, high = pl.ds(0, HALF), pl.ds(HALF, HALF)
    far, near = pl.ds(0, FAR), pl.ds(FAR, NZ - FAR)
    x_opp, x_a, x_bf, x_bn = {}, {}, {}, {}

    def send_opposite(j):
        x_opp[0, j] = send(chip.at[2, j, :, low], rx_opp.at[0, j], X_OPP + j, device(dx=1))
        x_opp[1, j] = send(chip.at[2, j, :, high], rx_opp.at[1, j], X_OPP + BLOCKS + j, device(dx=-1))

    def send_a(j):
        x_a[0, j] = send(chip.at[1, j, :, high], rx_a.at[0, j], X_A + j, device(dx=1))
        x_a[1, j] = send(chip.at[3, j, :, low], rx_a.at[1, j], X_A + BLOCKS + j, device(dx=-1))

    def send_b(j):
        for side, (k, part, step) in enumerate(((1, low, 1), (3, high, -1))):
            x_opp[side, j].wait_recv()
            for places, copies, base in ((far, x_bf, X_BF), (near, x_bn, X_BN)):
                total = chip[k, j, places, part].astype(F32) + rx_opp[side, j, places].astype(F32)
                tx_b[side, j, places] = total.astype(BF16)
                copies[side, j] = send(
                    tx_b.at[side, j, places], rx_b.at[side, j, places], base + side * BLOCKS + j, device(dx=step)
                )

    chip_sum(2, 0)
    send_opposite(0)
    chip_sum(1, 0)
    chip_sum(3, 0)
    send_a(0)
    chip_sum(2, 1)
    send_opposite(1)
    send_b(0)
    chip_sum(0, 0)
    chip_sum(1, 1)
    chip_sum(3, 1)
    send_a(1)
    send_b(1)
    chip_sum(0, 1)

    owners = [assign[t] for t in range(TASKS)]
    ranks = [
        sum(((owners[s] == owners[t]).astype(jnp.int32) for s in range(t)), jnp.int32(0)) for t in range(TASKS)
    ]
    for copy in slot_copies:
        copy.wait_recv()
    for t in range(TASKS):
        task_stats[t, my_rows] = slot_rows[owners[t], jnp.minimum(ranks[t], CAP - 1)]
    task_copies = [
        send(task_stats.at[:, my_rows], task_stats.at[:, my_rows], Y_TASK + d, device(dy=d))
        for d in (4, 3, 5, 2, 6, 1, 7)
    ]

    def x_total(j, places):
        bottom = chip[0, j, places, low].astype(F32) + rx_b[0, j, places].astype(F32) + rx_a[1, j, places].astype(F32)
        top = chip[0, j, places, high].astype(F32) + rx_a[0, j, places].astype(F32) + rx_b[1, j, places].astype(F32)
        return bottom, top

    z_far, z_near = {}, {}

    def far_stage(j):
        for side in range(2):
            x_a[side, j].wait_recv()
            x_bf[side, j].wait_recv()
        bottom, top = x_total(j, far)
        xs[j, far, low] = bottom.astype(BF16)
        xs[j, far, high] = top.astype(BF16)
        base = Z_FAR + 6 * j
        z_far[j] = [
            send(xs.at[j, 0, low], rz6.at[0, j], base, device(dz=3)),
            send(xs.at[j, 0, high], rz6.at[1, j], base + 1, device(dz=-3)),
            send(xs.at[j, 1], rz54.at[0, j, 0], base + 2, device(dz=2)),
            send(xs.at[j, 2], rz54.at[1, j, 0], base + 3, device(dz=-2)),
            send(xs.at[j, 3], rz54.at[0, j, 1], base + 4, device(dz=1)),
            send(xs.at[j, 4], rz54.at[1, j, 1], base + 5, device(dz=-1)),
        ]

    def near_stage(j):
        for side in range(2):
            x_bn[side, j].wait_recv()
        bottom, top = x_total(j, near)
        xs[j, near, low] = bottom.astype(BF16)
        xs[j, near, high] = top.astype(BF16)
        xs_own[j, low] = bottom[NZ - FAR - 1]
        xs_own[j, high] = top[NZ - FAR - 1]
        base = Z_NEAR + 6 * j
        z_near[j] = [
            send(xs.at[j, 7], rz_near.at[j, 2], base + 2, device(dz=2)),
            send(xs.at[j, 8], rz_near.at[j, 3], base + 3, device(dz=-2)),
            send(xs.at[j, 9], rz_near.at[j, 4], base + 4, device(dz=1)),
            send(xs.at[j, 10], rz_near.at[j, 5], base + 5, device(dz=-1)),
        ]

    def relay_stage(j):
        for copy in z_far[j]:
            copy.wait_recv()
        base = Z_NEAR + 6 * j
        for side, (part, rest, step) in enumerate(((low, high, 3), (high, low, -3))):
            total = (
                xs[j, 5 + side].astype(F32) + rz54[side, j, 0].astype(F32) + rz54[side, j, 1].astype(F32)
            )
            split = total[:HALF] if side == 0 else total[HALF:]
            plain = total[HALF:] if side == 0 else total[:HALF]
            tx_z[side, j, part] = (split + rz6[side, j].astype(F32)).astype(BF16)
            tx_z[side, j, rest] = plain.astype(BF16)
            z_near[j].append(send(tx_z.at[side, j], rz_near.at[j, side], base + side, device(dz=step)))

    grad_copies = {}

    def grad_stage(j):
        for copy in z_near[j]:
            copy.wait_recv()
        total = xs_own[j]
        for n in range(6):
            total = total + rz_near[j, n].astype(F32)
        grad[j, my_rows] = total.astype(BF16)
        grad_copies[j] = [
            send(grad.at[j, my_rows], grad.at[j, my_rows], Y_GRAD + NY * j + d, device(dy=d))
            for d in (4, 3, 5, 2, 6, 1, 7)
        ]

    far_stage(0)
    near_stage(0)
    far_stage(1)
    relay_stage(0)
    near_stage(1)
    relay_stage(1)
    grad_stage(0)
    grad_stage(1)

    for copy in task_copies:
        copy.wait_recv()
    for j in range(BLOCKS):
        for copy in grad_copies[j]:
            copy.wait_recv()
        block = grad[j]
        gram[2 * j] = dot(block, block, ((1,), (1,)))
        gram[2 * j + 1] = dot(block, block, ((0,), (0,)))
        left = inverse_root(DECAY_RATE * task_stats[2 * j].astype(F32) + gram[2 * j])
        right = inverse_root(DECAY_RATE * task_stats[2 * j + 1].astype(F32) + gram[2 * j + 1])
        half = dot(left, block).astype(BF16)
        pre = dot(half, right)
        pre_ref[...] = pre
        wide = block.astype(F32)
        scale = jnp.sqrt(jnp.sum(wide * wide) + NORM_EPSILON) / jnp.sqrt(jnp.sum(pre * pre) + NORM_EPSILON)
        upd_rows[j] = (pre_ref[my_rows] * scale).astype(BF16)

    for c in range(CAP):
        matches = [
            jnp.logical_and(owners[t] == y, ranks[t] == c).astype(jnp.int32) for t in range(TASKS)
        ]
        used = sum(matches, jnp.int32(0))
        task = sum((t * matches[t] for t in range(TASKS)), jnp.int32(0))
        fresh = DECAY_RATE * slots_in[c] + gram[jnp.minimum(task, TASKS - 1)]
        new_stats[c] = jnp.where(used > 0, fresh, jnp.zeros_like(fresh))
    out_copies = [
        pltpu.make_async_copy(new_stats, stats_out, local_sems.at[L_OUT]),
        pltpu.make_async_copy(upd_rows, update, local_sems.at[L_OUT + 1]),
    ]
    for copy in out_copies:
        copy.start()
    for copy in sent:
        copy.wait_send()
    for copy in out_copies:
        copy.wait()


def per_device(grad_parts, stats_in, assignment):
    parts = grad_parts.reshape(NX, NZ, NC, BLOCKS, ROWS, BS)
    slots = stats_in[0]
    assign = assignment.reshape(TASKS)
    any_space = pl.BlockSpec(memory_space=pl.ANY)
    update, stats_out = pl.pallas_call(
        kernel,
        out_shape=(
            jax.ShapeDtypeStruct((BLOCKS, ROWS, BS), BF16),
            jax.ShapeDtypeStruct((CAP, BS, BS), F32),
        ),
        in_specs=[any_space, any_space, pl.BlockSpec(memory_space=pltpu.SMEM)],
        out_specs=(any_space, any_space),
        scratch_shapes=[
            pltpu.VMEM((NX, BLOCKS, NZ, ROWS, BS), BF16),
            pltpu.VMEM((NX, BLOCKS, NZ, ROWS, BS), BF16),
            pltpu.VMEM((NX, BLOCKS, NZ, ROWS, BS), BF16),
            pltpu.VMEM((2, BLOCKS, NZ, HALF, BS), BF16),
            pltpu.VMEM((2, BLOCKS, NZ, HALF, BS), BF16),
            pltpu.VMEM((2, BLOCKS, NZ, HALF, BS), BF16),
            pltpu.VMEM((2, BLOCKS, NZ, HALF, BS), BF16),
            pltpu.VMEM((BLOCKS, NZ, ROWS, BS), BF16),
            pltpu.VMEM((BLOCKS, ROWS, BS), F32),
            pltpu.VMEM((2, BLOCKS, HALF, BS), BF16),
            pltpu.VMEM((2, BLOCKS, 2, ROWS, BS), BF16),
            pltpu.VMEM((2, BLOCKS, ROWS, BS), BF16),
            pltpu.VMEM((BLOCKS, 6, ROWS, BS), BF16),
            pltpu.VMEM((BLOCKS, BS, BS), BF16),
            pltpu.VMEM((CAP, BS, BS), F32),
            pltpu.VMEM((CAP, BS, BS), BF16),
            pltpu.VMEM((NY, CAP, ROWS, BS), BF16),
            pltpu.VMEM((TASKS, BS, BS), BF16),
            pltpu.VMEM((TASKS, BS, BS), F32),
            pltpu.VMEM((CAP, BS, BS), F32),
            pltpu.VMEM((BS, BS), F32),
            pltpu.VMEM((BLOCKS, ROWS, BS), BF16),
            pltpu.SemaphoreType.DMA((N_SEMS,)),
            pltpu.SemaphoreType.DMA((N_SEMS,)),
            pltpu.SemaphoreType.DMA((N_LOCAL,)),
        ],
        compiler_params=pltpu.CompilerParams(
            collective_id=0, has_side_effects=True, vmem_limit_bytes=60 * 1024 * 1024
        ),
        name="shampoo_step",
    )(parts, slots, assign)
    return update, stats_out[None]


def solution(mesh):
    in_specs = (P("dp", None, "owner", None), P("dp", "owner", None, None), P("dp", None, None))
    out_specs = (P("dp", "owner", None), P("dp", "owner", None, None))
    return jax.shard_map(
        per_device, mesh=mesh, in_specs=in_specs, out_specs=out_specs, check_vma=False
    )
```

time: 323 us -> 57.8 us (0.18)
  the two profiles are of different devices: /device:TPU:2 before, /device:TPU:1 now
where the time goes in v1:
time: 57.8 us; the launch traced here: 57.5 us
  Pallas kernels  53.7 us (93%)
  local copies, waits for them, and re-layouts  3.24 us (6%)
  between operations  0.64 us (1%)
    pallas_call x1, Pallas kernels, per_device(): pl.pallas_call(kernel, out_shape=(jax.ShapeDtypeStruct((BLOCKS, ROWS, BS)...  53.7 us
    unnamed x2, local copies, waits for them, and re-layouts  3.24 us

profile of v1, /device:TPU:1, one launch (start us, length us, event | category | flops | bytes accessed | tf_op | source)
XLA Modules:
  0.0 57.5 jit_solution(8681769601750087240)
XLA Ops:
  0.6 53.7 %shampoo_step.1 = (bf16[2,32,256]{2,1,0:T(8,128)(2,1)}, f32[2,256,256]{2,1,0:T(8,128)}) custom-call(bf16[4,12,2,2,32,256]{5,4,3,2,1,0:T(8,128)(2,1)} %bitcast.4, f32[2,256,256]{2,1,0:T(8,128)} %bitcast.6, s32[4]{0:T(128)} %bitcast.7), custom_call_target="tpu_custom_call" | custom-call | tf_op jit(solution)/shard_map/shampoo_step/pallas_call | solution.py:306
  54.3 1.4 %copy.7 = bf16[2,32,256]{2,1,0:T(8,128)(2,1)} copy(bf16[2,32,256]{2,1,0:T(8,128)(2,1)} %get-tuple-element.8) | data formatting | bytes 65536
  55.7 1.9 %copy.8 = f32[1,2,256,256]{3,2,1,0:T(8,128)} copy(f32[1,2,256,256]{3,2,1,0:T(8,128)} %bitcast.5) | data formatting | bytes 1048576

commit v2 on v0

v2 whole, which is shorter than its diff:
```python
import jax
import jax.numpy as jnp
from jax import lax
from jax.experimental import pallas as pl
from jax.experimental.pallas import tpu as pltpu
from jax.sharding import PartitionSpec as P

NX, NZ, NC, NY = 4, 12, 2, 8
BLOCKS = 2
TASKS = 4
CAP = 2
BS = 256
MID = BS // 2
ROWS = BS // NY
HALF = ROWS // 2
FAR = 5
DECAY_RATE = 0.95
NORM_EPSILON = 1e-06
MESH = pl.DeviceIdType.MESH
F32 = jnp.float32
BF16 = jnp.bfloat16

Z_ORDER = (6, 5, -5, 4, -4, 3, -3, 2, -2, 1, -1, 0)
Y_ORDER = (4, 3, 5, 2, 6, 1, 7)
UNITS = 4
X_UNITS = 3
LAST = UNITS - 1
GROUPS = (pl.ds(0, 2), pl.ds(2, 1))
CORE_ORDER = ((1, True), (3, True), (0, True), (1, False), (3, False), (0, False))

R_CORE_FAR, R_CORE_NEAR, R_X_FAR, R_X_NEAR, R_Z6, R_Z54, R_Z_NEAR, R_SLOT_TOP, R_SLOT_LOW = 0, 4, 8, 9, 11, 12, 13, 15, 16
R_TASK_TOP, R_TASK_LOW, R_GRAD, R_W6, R_W54, R_W_NEAR, R_W_X = 17, 18, 19, 21, 22, 23, 24
N_RECV = 25
S_CORE, S_X, S_Z6, S_Z54, S_SLOT_TOP, S_SLOT_LOW, S_TASK_TOP, S_TASK_LOW, S_GRAD, S_W6, S_W54, S_W_NEAR, S_W_X = range(13)
S_Z_NEAR = 13
N_SEND = 15
L_OWN_FAR, L_OWN_NEAR, L_STATS, L_STATS_OUT, L_UPDATE, L_ASSIGN = 0, 4, 8, 9, 10, 11
N_LOCAL = 12
IN_X, IN_Y, IN_Z = 0, 1, 4
N_IN = 6


def dot(left, right, dims=((1,), (0,))):
    return lax.dot_general(left, right, (dims, ((), ())), preferred_element_type=F32)


def inverse_root(stats):
    scale = 0.25 * lax.rsqrt(jnp.sum(stats * stats) + NORM_EPSILON)
    first = stats * scale
    first16 = first.astype(BF16)
    second = dot(first16, first16)
    second16 = second.astype(BF16)
    third = dot(first16, second16)
    third16 = third.astype(BF16)
    upper = dot((15.625 * first - 6.25 * second + third).astype(BF16), third16)
    rows = lax.broadcasted_iota(jnp.int32, (BS, BS), 0)
    columns = lax.broadcasted_iota(jnp.int32, (BS, BS), 1)
    diagonal = jnp.where(rows == columns, F32(1.5625), F32(0.0))
    root = diagonal - 4.3017578125 * first + 12.20703125 * second - 19.53125 * third + upper
    return root.astype(BF16)


def kernel(parts, stats_in, assign_in, update, stats_out,
           own, other, chip, rx_far, rx_near0, rx_near1,
           xs, xs_own, rz6, rz54, tx_z, rz_near0, rz_near1, rw6, rw54, tx_w, rw_near, ws, rw_x,
           grad, slots_in, slots16, slot_top, slot_low,
           task_top, task_low, task_stats, gram, new_stats, pre_ref, upd_rows,
           assign, send_sems, recv_sems, local_sems, in_sems):
    dp = lax.axis_index("dp")
    y = lax.axis_index("owner")
    x = dp // (NZ * NC)
    rest = dp - x * (NZ * NC)
    z = rest // NC
    core = rest - z * NC

    def around(position, step, size):
        moved = position + (step if step >= 0 else step + size)
        return moved - size * (moved >= size).astype(jnp.int32)

    x_at = [around(x, k, NX) for k in range(NX)]
    z_at = [around(z, step, NZ) for step in Z_ORDER]
    y_at = [around(y, d, NY) for d in range(NY)]

    def along_x(step):
        return (x_at[step % NX] * (NZ * NC) + rest, y)

    def along_z(step):
        return ((x * NZ + z_at[Z_ORDER.index(step)]) * NC + core, y)

    def along_y(d):
        return (dp, y_at[d])

    sibling = (dp + 1 - 2 * core, y)

    partners = [sibling, along_x(1), along_x(-1), along_z(1), along_z(-1), along_y(1), along_y(NY - 1)]
    barrier = pltpu.get_barrier_semaphore()
    for partner in partners:
        pl.semaphore_signal(barrier, inc=1, device_id=partner, device_id_type=MESH)

    def send(src, dst, send_number, recv_number, target):
        pltpu.make_async_remote_copy(
            src_ref=src, dst_ref=dst, send_sem=send_sems.at[send_number], recv_sem=recv_sems.at[recv_number],
            device_id=target, device_id_type=MESH,
        ).start()

    def wait(ref, sem):
        pltpu.make_async_copy(ref, ref, sem).wait()

    far, near = pl.ds(0, FAR), pl.ds(FAR, NZ - FAR)

    def load_own(k, is_far):
        base = L_OWN_FAR if is_far else L_OWN_NEAR
        for q in range(FAR) if is_far else range(FAR, NZ):
            pltpu.make_async_copy(
                parts.at[x_at[k], z_at[q], core], own.at[k, q], local_sems.at[base + k]
            ).start()

    def send_other(k, is_far):
        base = R_CORE_FAR if is_far else R_CORE_NEAR
        for q in range(FAR) if is_far else range(FAR, NZ):
            send(parts.at[x_at[k], z_at[q], 1 - core], other.at[k, q], S_CORE, base + k, sibling)

    def chip_sum(k, is_far):
        places = far if is_far else near
        wait(own.at[k, places], local_sems.at[(L_OWN_FAR if is_far else L_OWN_NEAR) + k])
        wait(other.at[k, places], recv_sems.at[(R_CORE_FAR if is_far else R_CORE_NEAR) + k])
        chip[k, places] = own[k, places] + other[k, places]

    load_own(2, True)
    stats_load = pltpu.make_async_copy(stats_in, slots_in, local_sems.at[L_STATS])
    stats_load.start()
    assign_load = pltpu.make_async_copy(assign_in, assign, local_sems.at[L_ASSIGN])
    assign_load.start()
    with jax.named_scope("barrier"):
        pl.semaphore_wait(barrier, len(partners))
    in_x = (along_x(1), along_x(-1))
    in_y = (along_y(1), along_y(NY - 1))
    in_z = (along_z(1), along_z(-1))

    def tell(number, neighbours):
        for neighbour in neighbours:
            pl.semaphore_signal(in_sems.at[number], inc=1, device_id=neighbour, device_id_type=MESH)

    def hear(number):
        pl.semaphore_wait(in_sems.at[number], 2)

    tell(IN_X, in_x)
    tell(IN_Y, in_y)
    tell(IN_Z, in_z)
    send_other(2, True)
    send_other(2, False)
    load_own(2, False)
    for k, is_far in CORE_ORDER:
        load_own(k, is_far)

    hear(IN_Y)
    tell(IN_Y + 1, in_y)
    hear(IN_Z)
    tell(IN_Z + 1, in_z)

    with jax.named_scope("chip_far"):
        chip_sum(2, True)
        for k, is_far in CORE_ORDER:
            send_other(k, is_far)
        hear(IN_X)
        send(chip.at[2, far, pl.ds(0, X_UNITS)], rx_far.at[0], S_X, R_X_FAR, along_x(2))
        chip_sum(1, True)
        send(chip.at[1, far, pl.ds(0, X_UNITS)], rx_far.at[1], S_X, R_X_FAR, along_x(1))
        chip_sum(3, True)
        send(chip.at[3, far, pl.ds(0, X_UNITS)], rx_far.at[2], S_X, R_X_FAR, along_x(-1))
        chip_sum(0, True)
    hear(IN_Y + 1)
    tell(IN_Y + 2, in_y)
    hear(IN_Z + 1)
    left, right = pl.ds(0, MID), pl.ds(MID, MID)
    with jax.named_scope("w_far"):
        for side, sign in enumerate((1, -1)):
            send(chip.at[:, 0, LAST, :, (left, right)[side]], rw6.at[side], S_W6, R_W6, along_z(3 * sign))
            send(chip.at[:, 1 + side, LAST], rw54.at[side, 0], S_W54, R_W54, along_z(2 * sign))
            send(chip.at[:, 3 + side, LAST], rw54.at[side, 1], S_W54, R_W54, along_z(sign))
    with jax.named_scope("chip_near"):
        chip_sum(2, False)
        chip_sum(1, False)
        chip_sum(3, False)
        for j, ref in enumerate((rx_near0, rx_near1)):
            for slot, k in enumerate((2, 1, 3)):
                send(chip.at[k, near, GROUPS[j]], ref.at[slot], S_X, R_X_NEAR + j, along_x(k if k < 3 else -1))
        chip_sum(0, False)
        for side, sign in enumerate((1, -1)):
            send(chip.at[:, 7 + side, LAST], rw_near.at[2 + side], S_W_NEAR, R_W_NEAR, along_z(2 * sign))
            send(chip.at[:, 9 + side, LAST], rw_near.at[4 + side], S_W_NEAR, R_W_NEAR, along_z(sign))
    hear(IN_Y + 2)

    my_eighth = pl.ds(pl.multiple_of(y * HALF, HALF), HALF)
    my_low = pl.ds(pl.multiple_of(MID + y * HALF, HALF), HALF)
    with jax.named_scope("slots"):
        stats_load.wait()
        slots16[...] = slots_in[...].astype(BF16)
        for d in Y_ORDER:
            top_rows = pl.ds(pl.multiple_of(y_at[d] * HALF, HALF), HALF)
            low_rows = pl.ds(pl.multiple_of(MID + y_at[d] * HALF, HALF), HALF)
            send(slots16.at[:, top_rows], slot_top.at[y], S_SLOT_TOP, R_SLOT_TOP, along_y(d))
            send(slots16.at[:, low_rows, right], slot_low.at[y], S_SLOT_LOW, R_SLOT_LOW, along_y(d))
        slot_top[y] = slots16[:, my_eighth]
        slot_low[y] = slots16[:, my_low, right]

    with jax.named_scope("z_far"):
        wait(rx_far, recv_sems.at[R_X_FAR])
        total = chip[0, far, pl.ds(0, X_UNITS)].astype(F32)
        for slot in range(3):
            total = total + rx_far[slot].astype(F32)
        xs[far] = total.astype(BF16)
        for side, sign in enumerate((1, -1)):
            send(xs.at[0, :, :, (left, right)[side]], rz6.at[side], S_Z6, R_Z6, along_z(3 * sign))
            send(xs.at[1 + side], rz54.at[side, 0], S_Z54, R_Z54, along_z(2 * sign))
            send(xs.at[3 + side], rz54.at[side, 1], S_Z54, R_Z54, along_z(sign))

    with jax.named_scope("w_relay"):
        wait(rw6, recv_sems.at[R_W6])
        wait(rw54, recv_sems.at[R_W54])
        for side, sign in enumerate((1, -1)):
            total = chip[:, 5 + side, LAST].astype(F32) + rw54[side, 0].astype(F32) + rw54[side, 1].astype(F32)
            part, other_part = (left, right) if side == 0 else (right, left)
            halves = (total[:, :, :MID], total[:, :, MID:])
            tx_w[side, :, :, part] = (halves[side] + rw6[side].astype(F32)).astype(BF16)
            tx_w[side, :, :, other_part] = halves[1 - side].astype(BF16)
            send(tx_w.at[side], rw_near.at[side], S_W_NEAR, R_W_NEAR, along_z(3 * sign))

    assign_load.wait()
    owners = [assign[t] for t in range(TASKS)]
    ranks = [
        sum(((owners[s] == owners[t]).astype(jnp.int32) for s in range(t)), jnp.int32(0)) for t in range(TASKS)
    ]
    with jax.named_scope("tasks"):
        wait(slot_top.at[pl.ds(0, NY - 1)], recv_sems.at[R_SLOT_TOP])
        wait(slot_low.at[pl.ds(0, NY - 1)], recv_sems.at[R_SLOT_LOW])
        for t in range(TASKS):
            rank = jnp.minimum(ranks[t], CAP - 1)
            task_top[t, my_eighth] = slot_top[owners[t], rank]
            task_low[t, my_eighth] = slot_low[owners[t], rank]
        for d in Y_ORDER:
            send(task_top.at[:, my_eighth], task_top.at[:, my_eighth], S_TASK_TOP, R_TASK_TOP, along_y(d))
            send(task_low.at[:, my_eighth], task_low.at[:, my_eighth], S_TASK_LOW, R_TASK_LOW, along_y(d))


    rz_near = (rz_near0, rz_near1)
    rx_near = (rx_near0, rx_near1)

    def z_near(j):
        wait(rx_near[j], recv_sems.at[R_X_NEAR + j])
        total = chip[0, near, GROUPS[j]].astype(F32)
        for slot in range(3):
            total = total + rx_near[j][slot].astype(F32)
        xs[near, GROUPS[j]] = total.astype(BF16)
        xs_own[GROUPS[j]] = total[NZ - FAR - 1]
        for side, sign in enumerate((1, -1)):
            send(xs.at[7 + side, GROUPS[j]], rz_near[j].at[2 + side], S_Z_NEAR + j, R_Z_NEAR + j, along_z(2 * sign))
            send(xs.at[9 + side, GROUPS[j]], rz_near[j].at[4 + side], S_Z_NEAR + j, R_Z_NEAR + j, along_z(sign))

    def z_relay():
        for side, sign in enumerate((1, -1)):
            total = xs[5 + side].astype(F32) + rz54[side, 0].astype(F32) + rz54[side, 1].astype(F32)
            part, other_part = (left, right) if side == 0 else (right, left)
            halves = (total[:, :, :MID], total[:, :, MID:])
            tx_z[side, :, :, part] = (halves[side] + rz6[side].astype(F32)).astype(BF16)
            tx_z[side, :, :, other_part] = halves[1 - side].astype(BF16)
        for j in range(BLOCKS):
            for side, sign in enumerate((1, -1)):
                send(tx_z.at[side, GROUPS[j]], rz_near[j].at[side], S_Z_NEAR + j, R_Z_NEAR + j, along_z(3 * sign))

    my_rows = pl.ds(pl.multiple_of(y * ROWS, ROWS), ROWS)
    my_last = pl.ds(pl.multiple_of(y * ROWS + HALF, HALF), HALF)

    def z_total(j):
        wait(rz_near[j], recv_sems.at[R_Z_NEAR + j])
        total = xs_own[GROUPS[j]]
        for n in range(6):
            total = total + rz_near[j][n].astype(F32)
        return total

    def gather(j):
        for d in Y_ORDER:
            send(grad.at[j, my_rows], grad.at[j, my_rows], S_GRAD, R_GRAD + j, along_y(d))

    with jax.named_scope("z_near0"):
        z_near(0)
    with jax.named_scope("z_near1"):
        z_near(1)
    with jax.named_scope("w_x"):
        wait(rw_near, recv_sems.at[R_W_NEAR])
        w_total = chip[:, NZ - 1, LAST].astype(F32)
        for n in range(6):
            w_total = w_total + rw_near[n].astype(F32)
        ws[...] = w_total.astype(BF16)
        for slot, k in enumerate((2, 1, 3)):
            send(ws.at[k], rw_x.at[slot], S_W_X, R_W_X, along_x(k if k < 3 else -1))
    with jax.named_scope("relay"):
        wait(rz6, recv_sems.at[R_Z6])
        wait(rz54, recv_sems.at[R_Z54])
        z_relay()
    with jax.named_scope("gather0"):
        grad[0, my_rows] = z_total(0).reshape(ROWS, BS).astype(BF16)
        gather(0)
    with jax.named_scope("gather1"):
        grad[1, pl.ds(pl.multiple_of(y * ROWS, ROWS), HALF)] = z_total(1)[0].astype(BF16)
        wait(rw_x, recv_sems.at[R_W_X])
        last = w_total[0]
        for slot in range(3):
            last = last + rw_x[slot].astype(F32)
        grad[1, my_last] = last.astype(BF16)
        gather(1)
    with jax.named_scope("task_wait"):
        wait(task_top.at[:, pl.ds(0, MID - HALF)], recv_sems.at[R_TASK_TOP])
        wait(task_low.at[:, pl.ds(0, MID - HALF)], recv_sems.at[R_TASK_LOW])
    with jax.named_scope("unfold"):
        for t in range(TASKS):
            top = DECAY_RATE * task_top[t].astype(F32)
            task_stats[t, pl.ds(0, MID)] = top
            task_stats[t, right, pl.ds(0, MID)] = top[:, MID:].T
            task_stats[t, right, right] = DECAY_RATE * task_low[t].astype(F32)

    def grams(j):
        block = grad[j]
        gram[2 * j] = dot(block, block, ((1,), (1,)))
        gram[2 * j + 1] = dot(block, block, ((0,), (0,)))

    def precondition(j):
        block = grad[j]
        left = inverse_root(task_stats[2 * j] + gram[2 * j])
        right_root = inverse_root(task_stats[2 * j + 1] + gram[2 * j + 1])
        half = dot(left, block).astype(BF16)
        pre = dot(half, right_root)
        pre_ref[...] = pre
        wide = block.astype(F32)
        scale = jnp.sqrt(jnp.sum(wide * wide) + NORM_EPSILON) / jnp.sqrt(jnp.sum(pre * pre) + NORM_EPSILON)
        upd_rows[j] = (pre_ref[my_rows] * scale).astype(BF16)

    with jax.named_scope("grad_wait0"):
        wait(grad.at[0, pl.ds(0, BS - ROWS)], recv_sems.at[R_GRAD])
    grams(0)
    precondition(0)
    with jax.named_scope("grad_wait1"):
        wait(grad.at[1, pl.ds(0, BS - ROWS)], recv_sems.at[R_GRAD + 1])
    grams(1)
    with jax.named_scope("stats_out"):
        for c in range(CAP):
            matches = [
                jnp.logical_and(owners[t] == y, ranks[t] == c).astype(jnp.int32) for t in range(TASKS)
            ]
            used = sum(matches, jnp.int32(0))
            task = sum((t * matches[t] for t in range(TASKS)), jnp.int32(0))
            fresh = DECAY_RATE * slots_in[c] + gram[jnp.minimum(task, TASKS - 1)]
            new_stats[c] = jnp.where(used > 0, fresh, jnp.zeros_like(fresh))
        stats_copy = pltpu.make_async_copy(new_stats, stats_out, local_sems.at[L_STATS_OUT])
        stats_copy.start()
    precondition(1)
    update_copy = pltpu.make_async_copy(upd_rows, update, local_sems.at[L_UPDATE])
    update_copy.start()
    with jax.named_scope("sent"):
        wait(own, send_sems.at[S_CORE])
        wait(chip.at[pl.ds(0, 3), :, pl.ds(0, X_UNITS)], send_sems.at[S_X])
        wait(rz6, send_sems.at[S_Z6])
        wait(rz54, send_sems.at[S_Z54])
        wait(rz_near0, send_sems.at[S_Z_NEAR])
        wait(rz_near1, send_sems.at[S_Z_NEAR + 1])
        wait(rw6, send_sems.at[S_W6])
        wait(rw54, send_sems.at[S_W54])
        wait(rw_near, send_sems.at[S_W_NEAR])
        wait(rw_x, send_sems.at[S_W_X])
        wait(slot_top.at[pl.ds(0, NY - 1)], send_sems.at[S_SLOT_TOP])
        wait(slot_low.at[pl.ds(0, NY - 1)], send_sems.at[S_SLOT_LOW])
        wait(task_top.at[:, pl.ds(0, MID - HALF)], send_sems.at[S_TASK_TOP])
        wait(task_low.at[:, pl.ds(0, MID - HALF)], send_sems.at[S_TASK_LOW])
        wait(grad.at[:, pl.ds(0, BS - ROWS)], send_sems.at[S_GRAD])
    with jax.named_scope("out"):
        stats_copy.wait()
        update_copy.wait()


def write_out(update_in, stats_in, update, stats_out):
    update[...] = update_in[...]
    stats_out[...] = stats_in[...]


def per_device(grad_parts, stats_in, assignment):
    parts = grad_parts.reshape(NX, NZ, NC, UNITS, HALF, BS)
    slots = stats_in[0]
    assign = assignment.reshape(TASKS)
    any_space = pl.BlockSpec(memory_space=pl.ANY)
    update, stats_out = pl.pallas_call(
        kernel,
        out_shape=(
            jax.ShapeDtypeStruct((BLOCKS, ROWS, BS), BF16),
            jax.ShapeDtypeStruct((CAP, BS, BS), F32),
        ),
        in_specs=[any_space, any_space, any_space],
        out_specs=(any_space, any_space),
        scratch_shapes=[
            pltpu.VMEM((NX, NZ, UNITS, HALF, BS), BF16),
            pltpu.VMEM((NX, NZ, UNITS, HALF, BS), BF16),
            pltpu.VMEM((NX, NZ, UNITS, HALF, BS), BF16),
            pltpu.VMEM((3, FAR, X_UNITS, HALF, BS), BF16),
            pltpu.VMEM((3, NZ - FAR, 2, HALF, BS), BF16),
            pltpu.VMEM((3, NZ - FAR, 1, HALF, BS), BF16),
            pltpu.VMEM((NZ, X_UNITS, HALF, BS), BF16),
            pltpu.VMEM((X_UNITS, HALF, BS), F32),
            pltpu.VMEM((2, X_UNITS, HALF, MID), BF16),
            pltpu.VMEM((2, 2, X_UNITS, HALF, BS), BF16),
            pltpu.VMEM((2, X_UNITS, HALF, BS), BF16),
            pltpu.VMEM((6, 2, HALF, BS), BF16),
            pltpu.VMEM((6, 1, HALF, BS), BF16),
            pltpu.VMEM((2, NX, HALF, MID), BF16),
            pltpu.VMEM((2, 2, NX, HALF, BS), BF16),
            pltpu.VMEM((2, NX, HALF, BS), BF16),
            pltpu.VMEM((6, NX, HALF, BS), BF16),
            pltpu.VMEM((NX, HALF, BS), BF16),
            pltpu.VMEM((3, HALF, BS), BF16),
            pltpu.VMEM((BLOCKS, BS, BS), BF16),
            pltpu.VMEM((CAP, BS, BS), F32),
            pltpu.VMEM((CAP, BS, BS), BF16),
            pltpu.VMEM((NY, CAP, HALF, BS), BF16),
            pltpu.VMEM((NY, CAP, HALF, MID), BF16),
            pltpu.VMEM((TASKS, MID, BS), BF16),
            pltpu.VMEM((TASKS, MID, MID), BF16),
            pltpu.VMEM((TASKS, BS, BS), F32),
            pltpu.VMEM((TASKS, BS, BS), F32),
            pltpu.VMEM((CAP, BS, BS), F32),
            pltpu.VMEM((BS, BS), F32),
            pltpu.VMEM((BLOCKS, ROWS, BS), BF16),
            pltpu.SMEM((TASKS,), jnp.int32),
            pltpu.SemaphoreType.DMA((N_SEND,)),
            pltpu.SemaphoreType.DMA((N_RECV,)),
            pltpu.SemaphoreType.DMA((N_LOCAL,)),
            pltpu.SemaphoreType.REGULAR((N_IN,)),
        ],
        compiler_params=pltpu.CompilerParams(
            collective_id=0, has_side_effects=True, vmem_limit_bytes=60 * 1024 * 1024
        ),
        name="shampoo_step",
    )(parts, slots, assign)
    update, stats_out = pl.pallas_call(
        write_out,
        out_shape=(
            jax.ShapeDtypeStruct((BLOCKS, ROWS, BS), BF16),
            jax.ShapeDtypeStruct((CAP, BS, BS), F32),
        ),
        name="write_out",
    )(update, stats_out)
    return update, stats_out[None]


def solution(mesh):
    in_specs = (P("dp", None, "owner", None), P("dp", "owner", None, None), P("dp", None, None))
    out_specs = (P("dp", "owner", None), P("dp", "owner", None, None))
    return jax.shard_map(
        per_device, mesh=mesh, in_specs=in_specs, out_specs=out_specs, check_vma=False
    )
```

time: 323 us -> 51.6 us (0.16)
  the two profiles are of different devices: /device:TPU:2 before, /device:TPU:8 now
where the time goes in v2:
time: 51.6 us; the launch traced here: 51.4 us
  Pallas kernels  50.7 us (98%)
  between operations  0.64 us (1%)
    pallas_call x1, Pallas kernels, per_device(): pl.pallas_call(kernel, out_shape=(jax.ShapeDtypeStruct((BLOCKS, ROWS, BS)...  48.8 us
    pallas_call x1, Pallas kernels, per_device(): pl.pallas_call(write_out, out_shape=(jax.ShapeDtypeStruct((BLOCKS, ROWS,...  1.89 us

profile of v2, /device:TPU:8, one launch (start us, length us, event | category | flops | bytes accessed | tf_op | source)
XLA Modules:
  0.0 51.4 jit_solution(11426492819289210694)
XLA Ops:
  0.6 48.8 %shampoo_step.1 = (bf16[2,32,256]{2,1,0:T(8,128)(2,1)}, f32[2,256,256]{2,1,0:T(8,128)}) custom-call(bf16[4,12,2,4,16,256]{5,4,3,2,1,0:T(8,128)(2,1)} %bitcast.4, f32[2,256,256]{2,1,0:T(8,128)} %bitcast.5, s32[4]{0:T(128)} %bitcast.6), custom_call_target="tpu_custom_call" | custom-call | tf_op jit(solution)/shard_map/shampoo_step/pallas_call | solution.py:390
  49.5 1.9 %write_out.1 = (bf16[2,32,256]{2,1,0:T(8,128)(2,1)}, f32[2,256,256]{2,1,0:T(8,128)}) custom-call(bf16[2,32,256]{2,1,0:T(8,128)(2,1)} %get-tuple-element.6.update_in, f32[2,256,256]{2,1,0:T(8,128)} %get-tuple-element.7.stats_in), custom_call_target="tpu_custom_call" | custom-call | tf_op jit(solution)/shard_map/write_out/pallas_call | solution.py:441

commit v3 on v2

--- a/solution.py
+++ b/solution.py
@@ -26,7 +26,6 @@
 X_UNITS = 3
 LAST = UNITS - 1
 GROUPS = (pl.ds(0, 2), pl.ds(2, 1))
-CORE_ORDER = ((1, True), (3, True), (0, True), (1, False), (3, False), (0, False))
 
 R_CORE_FAR, R_CORE_NEAR, R_X_FAR, R_X_NEAR, R_Z6, R_Z54, R_Z_NEAR, R_SLOT_TOP, R_SLOT_LOW = 0, 4, 8, 9, 11, 12, 13, 15, 16
 R_TASK_TOP, R_TASK_LOW, R_GRAD, R_W6, R_W54, R_W_NEAR, R_W_X = 17, 18, 19, 21, 22, 23, 24
@@ -147,21 +146,22 @@
     tell(IN_X, in_x)
     tell(IN_Y, in_y)
     tell(IN_Z, in_z)
-    send_other(2, True)
-    send_other(2, False)
-    load_own(2, False)
-    for k, is_far in CORE_ORDER:
-        load_own(k, is_far)
+    for k in (2, 1, 3, 0):
+        send_other(k, True)
+    for k in (1, 3, 0):
+        load_own(k, True)
+    for k in (2, 1, 3, 0):
+        load_own(k, False)
 
     hear(IN_Y)
     tell(IN_Y + 1, in_y)
     hear(IN_Z)
     tell(IN_Z + 1, in_z)
+    for k in (2, 1, 3, 0):
+        send_other(k, False)
 
     with jax.named_scope("chip_far"):
         chip_sum(2, True)
-        for k, is_far in CORE_ORDER:
-            send_other(k, is_far)
         hear(IN_X)
         send(chip.at[2, far, pl.ds(0, X_UNITS)], rx_far.at[0], S_X, R_X_FAR, along_x(2))
         chip_sum(1, True)
@@ -257,16 +257,16 @@
             send(xs.at[7 + side, GROUPS[j]], rz_near[j].at[2 + side], S_Z_NEAR + j, R_Z_NEAR + j, along_z(2 * sign))
             send(xs.at[9 + side, GROUPS[j]], rz_near[j].at[4 + side], S_Z_NEAR + j, R_Z_NEAR + j, along_z(sign))
 
-    def z_relay():
-        for side, sign in enumerate((1, -1)):
-            total = xs[5 + side].astype(F32) + rz54[side, 0].astype(F32) + rz54[side, 1].astype(F32)
+    def z_relay(j):
+        units = GROUPS[j]
+        for side, sign in enumerate((1, -1)):
+            total = xs[5 + side, units].astype(F32)
+            total = total + rz54[side, 0, units].astype(F32) + rz54[side, 1, units].astype(F32)
             part, other_part = (left, right) if side == 0 else (right, left)
             halves = (total[:, :, :MID], total[:, :, MID:])
-            tx_z[side, :, :, part] = (halves[side] + rz6[side].astype(F32)).astype(BF16)
-            tx_z[side, :, :, other_part] = halves[1 - side].astype(BF16)
-        for j in range(BLOCKS):
-            for side, sign in enumerate((1, -1)):
-                send(tx_z.at[side, GROUPS[j]], rz_near[j].at[side], S_Z_NEAR + j, R_Z_NEAR + j, along_z(3 * sign))
+            tx_z[side, units, :, part] = (halves[side] + rz6[side, units].astype(F32)).astype(BF16)
+            tx_z[side, units, :, other_part] = halves[1 - side].astype(BF16)
+            send(tx_z.at[side, units], rz_near[j].at[side], S_Z_NEAR + j, R_Z_NEAR + j, along_z(3 * sign))
 
     my_rows = pl.ds(pl.multiple_of(y * ROWS, ROWS), ROWS)
     my_last = pl.ds(pl.multiple_of(y * ROWS + HALF, HALF), HALF)
@@ -284,8 +284,14 @@
 
     with jax.named_scope("z_near0"):
         z_near(0)
+    with jax.named_scope("relay0"):
+        wait(rz6, recv_sems.at[R_Z6])
+        wait(rz54, recv_sems.at[R_Z54])
+        z_relay(0)
     with jax.named_scope("z_near1"):
         z_near(1)
+    with jax.named_scope("relay1"):
+        z_relay(1)
     with jax.named_scope("w_x"):
         wait(rw_near, recv_sems.at[R_W_NEAR])
         w_total = chip[:, NZ - 1, LAST].astype(F32)
@@ -294,10 +300,6 @@
         ws[...] = w_total.astype(BF16)
         for slot, k in enumerate((2, 1, 3)):
             send(ws.at[k], rw_x.at[slot], S_W_X, R_W_X, along_x(k if k < 3 else -1))
-    with jax.named_scope("relay"):
-        wait(rz6, recv_sems.at[R_Z6])
-        wait(rz54, recv_sems.at[R_Z54])
-        z_relay()
     with jax.named_scope("gather0"):
         grad[0, my_rows] = z_total(0).reshape(ROWS, BS).astype(BF16)
         gather(0)

time: 51.6 us -> 49.9 us (0.967)
  Pallas kernels: 50.7 us -> 49 us
    pallas_call x1, Pallas kernels: 48.8 us -> 47.1 us  [per_device(): pl.pallas_call(kernel, out_shape=(jax.ShapeDtypeStruct((BLOCKS, ROWS, BS)...]
where the time goes in v3:
time: 49.9 us; the launch traced here: 49.7 us
  Pallas kernels  49 us (98%)
  between operations  0.64 us (1%)
    pallas_call x1, Pallas kernels, per_device(): pl.pallas_call(kernel, out_shape=(jax.ShapeDtypeStruct((BLOCKS, ROWS, BS)...  47.1 us
    pallas_call x1, Pallas kernels, per_device(): pl.pallas_call(write_out, out_shape=(jax.ShapeDtypeStruct((BLOCKS, ROWS,...  1.89 us

profile of v3, /device:TPU:8, one launch (start us, length us, event | category | flops | bytes accessed | tf_op | source)
XLA Modules:
  0.0 49.7 jit_solution(1430451946007073424)
XLA Ops:
  0.6 47.1 %shampoo_step.1 = (bf16[2,32,256]{2,1,0:T(8,128)(2,1)}, f32[2,256,256]{2,1,0:T(8,128)}) custom-call(bf16[4,12,2,4,16,256]{5,4,3,2,1,0:T(8,128)(2,1)} %bitcast.4, f32[2,256,256]{2,1,0:T(8,128)} %bitcast.5, s32[4]{0:T(128)} %bitcast.6), custom_call_target="tpu_custom_call" | custom-call | tf_op jit(solution)/shard_map/shampoo_step/pallas_call | solution.py:392
  47.8 1.9 %write_out.1 = (bf16[2,32,256]{2,1,0:T(8,128)(2,1)}, f32[2,256,256]{2,1,0:T(8,128)}) custom-call(bf16[2,32,256]{2,1,0:T(8,128)(2,1)} %get-tuple-element.6.update_in, f32[2,256,256]{2,1,0:T(8,128)} %get-tuple-element.7.stats_in), custom_call_target="tpu_custom_call" | custom-call | tf_op jit(solution)/shard_map/write_out/pallas_call | solution.py:443

commit v4 on v3

--- a/solution.py
+++ b/solution.py
@@ -27,12 +27,12 @@
 LAST = UNITS - 1
 GROUPS = (pl.ds(0, 2), pl.ds(2, 1))
 
-R_CORE_FAR, R_CORE_NEAR, R_X_FAR, R_X_NEAR, R_Z6, R_Z54, R_Z_NEAR, R_SLOT_TOP, R_SLOT_LOW = 0, 4, 8, 9, 11, 12, 13, 15, 16
-R_TASK_TOP, R_TASK_LOW, R_GRAD, R_W6, R_W54, R_W_NEAR, R_W_X = 17, 18, 19, 21, 22, 23, 24
-N_RECV = 25
-S_CORE, S_X, S_Z6, S_Z54, S_SLOT_TOP, S_SLOT_LOW, S_TASK_TOP, S_TASK_LOW, S_GRAD, S_W6, S_W54, S_W_NEAR, S_W_X = range(13)
-S_Z_NEAR = 13
-N_SEND = 15
+R_CORE_FAR, R_CORE_NEAR, R_X_FAR, R_X_NEAR, R_Z6, R_Z54, R_Z_NEAR, R_SLOT_TOP, R_SLOT_LOW = 0, 4, 8, 9, 11, 13, 15, 17, 18
+R_TASK_TOP, R_TASK_LOW, R_GRAD, R_W6, R_W54, R_W_NEAR, R_W_X = 19, 20, 21, 23, 24, 25, 26
+N_RECV = 27
+S_CORE, S_X, S_X_FAR, S_SLOT_TOP, S_SLOT_LOW, S_TASK_TOP, S_TASK_LOW, S_GRAD, S_W6, S_W54, S_W_NEAR, S_W_X = range(12)
+S_Z6, S_Z54, S_Z_NEAR = 12, 14, 16
+N_SEND = 18
 L_OWN_FAR, L_OWN_NEAR, L_STATS, L_STATS_OUT, L_UPDATE, L_ASSIGN = 0, 4, 8, 9, 10, 11
 N_LOCAL = 12
 IN_X, IN_Y, IN_Z = 0, 1, 4
@@ -45,11 +45,12 @@
 
 def inverse_root(stats):
     scale = 0.25 * lax.rsqrt(jnp.sum(stats * stats) + NORM_EPSILON)
+    stats16 = stats.astype(BF16)
+    square = dot(stats16, stats16)
+    cube = dot(stats16, square.astype(BF16))
     first = stats * scale
-    first16 = first.astype(BF16)
-    second = dot(first16, first16)
-    second16 = second.astype(BF16)
-    third = dot(first16, second16)
+    second = square * (scale * scale)
+    third = cube * (scale * scale * scale)
     third16 = third.astype(BF16)
     upper = dot((15.625 * first - 6.25 * second + third).astype(BF16), third16)
     rows = lax.broadcasted_iota(jnp.int32, (BS, BS), 0)
@@ -61,7 +62,7 @@
 
 def kernel(parts, stats_in, assign_in, update, stats_out,
            own, other, chip, rx_far, rx_near0, rx_near1,
-           xs, xs_own, rz6, rz54, tx_z, rz_near0, rz_near1, rw6, rw54, tx_w, rw_near, ws, rw_x,
+           xs, xs_own, rz6_0, rz6_1, rz54_0, rz54_1, tx_z, rz_near0, rz_near1, rw6, rw54, tx_w, rw_near, ws, rw_x,
            grad, slots_in, slots16, slot_top, slot_low,
            task_top, task_low, task_stats, gram, new_stats, pre_ref, upd_rows,
            assign, send_sems, recv_sems, local_sems, in_sems):
@@ -152,22 +153,22 @@
         load_own(k, True)
     for k in (2, 1, 3, 0):
         load_own(k, False)
+    for k in (2, 1, 3, 0):
+        send_other(k, False)
 
     hear(IN_Y)
     tell(IN_Y + 1, in_y)
     hear(IN_Z)
     tell(IN_Z + 1, in_z)
-    for k in (2, 1, 3, 0):
-        send_other(k, False)
 
     with jax.named_scope("chip_far"):
         chip_sum(2, True)
         hear(IN_X)
-        send(chip.at[2, far, pl.ds(0, X_UNITS)], rx_far.at[0], S_X, R_X_FAR, along_x(2))
+        send(chip.at[2, far, pl.ds(0, X_UNITS)], rx_far.at[0], S_X_FAR, R_X_FAR, along_x(2))
         chip_sum(1, True)
-        send(chip.at[1, far, pl.ds(0, X_UNITS)], rx_far.at[1], S_X, R_X_FAR, along_x(1))
+        send(chip.at[1, far, pl.ds(0, X_UNITS)], rx_far.at[1], S_X_FAR, R_X_FAR, along_x(1))
         chip_sum(3, True)
-        send(chip.at[3, far, pl.ds(0, X_UNITS)], rx_far.at[2], S_X, R_X_FAR, along_x(-1))
+        send(chip.at[3, far, pl.ds(0, X_UNITS)], rx_far.at[2], S_X_FAR, R_X_FAR, along_x(-1))
         chip_sum(0, True)
     hear(IN_Y + 1)
     tell(IN_Y + 2, in_y)
@@ -182,9 +183,6 @@
         chip_sum(2, False)
         chip_sum(1, False)
         chip_sum(3, False)
-        for j, ref in enumerate((rx_near0, rx_near1)):
-            for slot, k in enumerate((2, 1, 3)):
-                send(chip.at[k, near, GROUPS[j]], ref.at[slot], S_X, R_X_NEAR + j, along_x(k if k < 3 else -1))
         chip_sum(0, False)
         for side, sign in enumerate((1, -1)):
             send(chip.at[:, 7 + side, LAST], rw_near.at[2 + side], S_W_NEAR, R_W_NEAR, along_z(2 * sign))
@@ -204,17 +202,29 @@
         slot_top[y] = slots16[:, my_eighth]
         slot_low[y] = slots16[:, my_low, right]
 
+    with jax.named_scope("x_near"):
+        wait(rx_far, send_sems.at[S_X_FAR])
+        for j, ref in enumerate((rx_near0, rx_near1)):
+            for slot, k in enumerate((2, 1, 3)):
+                send(chip.at[k, near, GROUPS[j]], ref.at[slot], S_X, R_X_NEAR + j, along_x(k if k < 3 else -1))
+
+    rz6, rz54 = (rz6_0, rz6_1), (rz54_0, rz54_1)
+
     with jax.named_scope("z_far"):
         wait(rx_far, recv_sems.at[R_X_FAR])
         total = chip[0, far, pl.ds(0, X_UNITS)].astype(F32)
         for slot in range(3):
             total = total + rx_far[slot].astype(F32)
         xs[far] = total.astype(BF16)
-        for side, sign in enumerate((1, -1)):
-            send(xs.at[0, :, :, (left, right)[side]], rz6.at[side], S_Z6, R_Z6, along_z(3 * sign))
-            send(xs.at[1 + side], rz54.at[side, 0], S_Z54, R_Z54, along_z(2 * sign))
-            send(xs.at[3 + side], rz54.at[side, 1], S_Z54, R_Z54, along_z(sign))
-
+
+    def send_far(j):
+        units = GROUPS[j]
+        for side, sign in enumerate((1, -1)):
+            send(xs.at[0, units, :, (left, right)[side]], rz6[j].at[side], S_Z6 + j, R_Z6 + j, along_z(3 * sign))
+            send(xs.at[1 + side, units], rz54[j].at[side, 0], S_Z54 + j, R_Z54 + j, along_z(2 * sign))
+            send(xs.at[3 + side, units], rz54[j].at[side, 1], S_Z54 + j, R_Z54 + j, along_z(sign))
+
+    send_far(0)
     with jax.named_scope("w_relay"):
         wait(rw6, recv_sems.at[R_W6])
         wait(rw54, recv_sems.at[R_W54])
@@ -225,6 +235,8 @@
             tx_w[side, :, :, part] = (halves[side] + rw6[side].astype(F32)).astype(BF16)
             tx_w[side, :, :, other_part] = halves[1 - side].astype(BF16)
             send(tx_w.at[side], rw_near.at[side], S_W_NEAR, R_W_NEAR, along_z(3 * sign))
+
+    send_far(1)
 
     assign_load.wait()
     owners = [assign[t] for t in range(TASKS)]
@@ -261,10 +273,10 @@
         units = GROUPS[j]
         for side, sign in enumerate((1, -1)):
             total = xs[5 + side, units].astype(F32)
-            total = total + rz54[side, 0, units].astype(F32) + rz54[side, 1, units].astype(F32)
+            total = total + rz54[j][side, 0].astype(F32) + rz54[j][side, 1].astype(F32)
             part, other_part = (left, right) if side == 0 else (right, left)
             halves = (total[:, :, :MID], total[:, :, MID:])
-            tx_z[side, units, :, part] = (halves[side] + rz6[side, units].astype(F32)).astype(BF16)
+            tx_z[side, units, :, part] = (halves[side] + rz6[j][side].astype(F32)).astype(BF16)
             tx_z[side, units, :, other_part] = halves[1 - side].astype(BF16)
             send(tx_z.at[side, units], rz_near[j].at[side], S_Z_NEAR + j, R_Z_NEAR + j, along_z(3 * sign))
 
@@ -285,12 +297,14 @@
     with jax.named_scope("z_near0"):
         z_near(0)
     with jax.named_scope("relay0"):
-        wait(rz6, recv_sems.at[R_Z6])
-        wait(rz54, recv_sems.at[R_Z54])
+        wait(rz6[0], recv_sems.at[R_Z6])
+        wait(rz54[0], recv_sems.at[R_Z54])
         z_relay(0)
     with jax.named_scope("z_near1"):
         z_near(1)
     with jax.named_scope("relay1"):
+        wait(rz6[1], recv_sems.at[R_Z6 + 1])
+        wait(rz54[1], recv_sems.at[R_Z54 + 1])
         z_relay(1)
     with jax.named_scope("w_x"):
         wait(rw_near, recv_sems.at[R_W_NEAR])
@@ -360,9 +374,10 @@
     update_copy.start()
     with jax.named_scope("sent"):
         wait(own, send_sems.at[S_CORE])
-        wait(chip.at[pl.ds(0, 3), :, pl.ds(0, X_UNITS)], send_sems.at[S_X])
-        wait(rz6, send_sems.at[S_Z6])
-        wait(rz54, send_sems.at[S_Z54])
+        wait(chip.at[pl.ds(0, 3), near, pl.ds(0, X_UNITS)], send_sems.at[S_X])
+        for j in range(BLOCKS):
+            wait(rz6[j], send_sems.at[S_Z6 + j])
+            wait(rz54[j], send_sems.at[S_Z54 + j])
         wait(rz_near0, send_sems.at[S_Z_NEAR])
         wait(rz_near1, send_sems.at[S_Z_NEAR + 1])
         wait(rw6, send_sems.at[S_W6])
@@ -406,8 +421,10 @@
             pltpu.VMEM((3, NZ - FAR, 1, HALF, BS), BF16),
             pltpu.VMEM((NZ, X_UNITS, HALF, BS), BF16),
             pltpu.VMEM((X_UNITS, HALF, BS), F32),
-            pltpu.VMEM((2, X_UNITS, HALF, MID), BF16),
-            pltpu.VMEM((2, 2, X_UNITS, HALF, BS), BF16),
+            pltpu.VMEM((2, 2, HALF, MID), BF16),
+            pltpu.VMEM((2, 1, HALF, MID), BF16),
+            pltpu.VMEM((2, 2, 2, HALF, BS), BF16),
+            pltpu.VMEM((2, 2, 1, HALF, BS), BF16),
             pltpu.VMEM((2, X_UNITS, HALF, BS), BF16),
             pltpu.VMEM((6, 2, HALF, BS), BF16),
             pltpu.VMEM((6, 1, HALF, BS), BF16),

time: 49.9 us -> 49.4 us (0.990)
  Pallas kernels: 49 us -> 48.5 us
    pallas_call x1, Pallas kernels: 47.1 us -> 46.6 us  [per_device(): pl.pallas_call(kernel, out_shape=(jax.ShapeDtypeStruct((BLOCKS, ROWS, BS)...]
where the time goes in v4:
time: 49.4 us; the launch traced here: 49.1 us
  Pallas kernels  48.5 us (98%)
  between operations  0.64 us (1%)
    pallas_call x1, Pallas kernels, per_device(): pl.pallas_call(kernel, out_shape=(jax.ShapeDtypeStruct((BLOCKS, ROWS, BS)...  46.6 us
    pallas_call x1, Pallas kernels, per_device(): pl.pallas_call(write_out, out_shape=(jax.ShapeDtypeStruct((BLOCKS, ROWS,...  1.89 us

profile of v4, /device:TPU:8, one launch (start us, length us, event | category | flops | bytes accessed | tf_op | source)
XLA Modules:
  0.0 49.1 jit_solution(1164886310729828953)
XLA Ops:
  0.6 46.6 %shampoo_step.1 = (bf16[2,32,256]{2,1,0:T(8,128)(2,1)}, f32[2,256,256]{2,1,0:T(8,128)}) custom-call(bf16[4,12,2,4,16,256]{5,4,3,2,1,0:T(8,128)(2,1)} %bitcast.4, f32[2,256,256]{2,1,0:T(8,128)} %bitcast.5, s32[4]{0:T(128)} %bitcast.6), custom_call_target="tpu_custom_call" | custom-call | tf_op jit(solution)/shard_map/shampoo_step/pallas_call | solution.py:407
  47.2 1.9 %write_out.1 = (bf16[2,32,256]{2,1,0:T(8,128)(2,1)}, f32[2,256,256]{2,1,0:T(8,128)}) custom-call(bf16[2,32,256]{2,1,0:T(8,128)(2,1)} %get-tuple-element.6.update_in, f32[2,256,256]{2,1,0:T(8,128)} %get-tuple-element.7.stats_in), custom_call_target="tpu_custom_call" | custom-call | tf_op jit(solution)/shard_map/write_out/pallas_call | solution.py:460

commit v5 on v4

--- a/solution.py
+++ b/solution.py
@@ -394,9 +394,15 @@
         update_copy.wait()
 
 
-def write_out(update_in, stats_in, update, stats_out):
-    update[...] = update_in[...]
-    stats_out[...] = stats_in[...]
+def write_out(update_in, stats_in, update, stats_out, sems):
+    copies = [
+        pltpu.make_async_copy(stats_in, stats_out, sems.at[0]),
+        pltpu.make_async_copy(update_in, update, sems.at[1]),
+    ]
+    for copy in copies:
+        copy.start()
+    for copy in copies:
+        copy.wait()
 
 
 def per_device(grad_parts, stats_in, assignment):
@@ -453,7 +459,7 @@
             pltpu.SemaphoreType.REGULAR((N_IN,)),
         ],
         compiler_params=pltpu.CompilerParams(
-            collective_id=0, has_side_effects=True, vmem_limit_bytes=60 * 1024 * 1024
+            collective_id=0, has_side_effects=True, vmem_limit_bytes=53 * 1024 * 1024
         ),
         name="shampoo_step",
     )(parts, slots, assign)
@@ -463,6 +469,10 @@
             jax.ShapeDtypeStruct((BLOCKS, ROWS, BS), BF16),
             jax.ShapeDtypeStruct((CAP, BS, BS), F32),
         ),
+        in_specs=[any_space, any_space],
+        out_specs=(any_space, any_space),
+        scratch_shapes=[pltpu.SemaphoreType.DMA((2,))],
+        compiler_params=pltpu.CompilerParams(vmem_limit_bytes=1024 * 1024),
         name="write_out",
     )(update, stats_out)
     return update, stats_out[None]

time: 49.4 us -> 48.5 us (0.982)
  Pallas kernels: 48.5 us -> 46.9 us
  local copies, waits for them, and re-layouts: 0 us -> 0.65 us
    pallas_call x1, Pallas kernels: 1.89 us -> 0.81 us  [per_device(): pl.pallas_call(write_out, out_shape=(jax.ShapeDtypeStruct((BLOCKS, ROWS,...]
    unnamed x0 -> x2, local copies, waits for them, and re-layouts: none -> 0.65 us
where the time goes in v5:
time: 48.5 us; the launch traced here: 48.2 us
  Pallas kernels  46.9 us (97%)
  local copies, waits for them, and re-layouts  0.65 us (1%)
  between operations  0.65 us (1%)
    pallas_call x1, Pallas kernels, per_device(): pl.pallas_call(kernel, out_shape=(jax.ShapeDtypeStruct((BLOCKS, ROWS, BS)...  46.1 us

profile of v5, /device:TPU:8, one launch (start us, length us, event | category | flops | bytes accessed | tf_op | source)
XLA Modules:
  0.0 48.2 jit_solution(4578766060949477590)
XLA Ops:
  0.6 0.0 copy-start
  0.6 0.6 %copy-done = s32[1,4,1]{1,2,0:T(1,128)S(1)} copy-done((s32[1,4,1]{1,2,0:T(1,128)S(1)}, s32[1,4,1]{1,2,0:T(1,128)}, u32[]{:S(2)}) %copy-start) | copy-done | bytes 40
  1.3 46.1 %shampoo_step.1 = (bf16[2,32,256]{2,1,0:T(8,128)(2,1)S(1)}, f32[2,256,256]{2,1,0:T(8,128)S(1)}) custom-call(bf16[4,12,2,4,16,256]{5,4,3,2,1,0:T(8,128)(2,1)} %bitcast.5, f32[2,256,256]{2,1,0:T(8,128)} %bitcast.6, s32[4]{0:T(128)S(1)} %bitcast.4), custom_call_target="tpu_custom_call" | custom-call | tf_op jit(solution)/shard_map/shampoo_step/pallas_call | solution.py:413
  47.4 0.8 %write_out.1 = (bf16[2,32,256]{2,1,0:T(8,128)(2,1)}, f32[2,256,256]{2,1,0:T(8,128)}) custom-call(bf16[2,32,256]{2,1,0:T(8,128)(2,1)S(1)} %get-tuple-element.6.update_in, f32[2,256,256]{2,1,0:T(8,128)S(1)} %get-tuple-element.7.stats_in), custom_call_target="tpu_custom_call" | custom-call | tf_op jit(solution)/shard_map/write_out/pallas_call | solution.py:466
Async XLA Ops:
  0.6 0.7 %copy-start = (s32[1,4,1]{1,2,0:T(1,128)S(1)}, s32[1,4,1]{1,2,0:T(1,128)}, u32[]{:S(2)}) copy-start(s32[1,4,1]{1,2,0:T(1,128)} %param.5) | copy-start | bytes 52

commit v6 on v5

--- a/solution.py
+++ b/solution.py
@@ -265,6 +265,8 @@
             total = total + rx_near[j][slot].astype(F32)
         xs[near, GROUPS[j]] = total.astype(BF16)
         xs_own[GROUPS[j]] = total[NZ - FAR - 1]
+
+    def z_direct(j):
         for side, sign in enumerate((1, -1)):
             send(xs.at[7 + side, GROUPS[j]], rz_near[j].at[2 + side], S_Z_NEAR + j, R_Z_NEAR + j, along_z(2 * sign))
             send(xs.at[9 + side, GROUPS[j]], rz_near[j].at[4 + side], S_Z_NEAR + j, R_Z_NEAR + j, along_z(sign))
@@ -300,12 +302,14 @@
         wait(rz6[0], recv_sems.at[R_Z6])
         wait(rz54[0], recv_sems.at[R_Z54])
         z_relay(0)
+        z_direct(0)
     with jax.named_scope("z_near1"):
         z_near(1)
     with jax.named_scope("relay1"):
         wait(rz6[1], recv_sems.at[R_Z6 + 1])
         wait(rz54[1], recv_sems.at[R_Z54 + 1])
         z_relay(1)
+        z_direct(1)
     with jax.named_scope("w_x"):
         wait(rw_near, recv_sems.at[R_W_NEAR])
         w_total = chip[:, NZ - 1, LAST].astype(F32)

time: 48.5 us -> 48.7 us (level)
  no operation moved by 1% of the time
where the time goes in v6:
time: 48.7 us; the launch traced here: 48.5 us
  Pallas kernels  47.2 us (97%)
  local copies, waits for them, and re-layouts  0.65 us (1%)
  between operations  0.65 us (1%)
    pallas_call x1, Pallas kernels, per_device(): pl.pallas_call(kernel, out_shape=(jax.ShapeDtypeStruct((BLOCKS, ROWS, BS)...  46.4 us

profile of v6, /device:TPU:8, one launch (start us, length us, event | category | flops | bytes accessed | tf_op | source)
XLA Modules:
  0.0 48.5 jit_solution(1773488890617684583)
XLA Ops:
  0.6 0.0 copy-start
  0.6 0.6 %copy-done = s32[1,4,1]{1,2,0:T(1,128)S(1)} copy-done((s32[1,4,1]{1,2,0:T(1,128)S(1)}, s32[1,4,1]{1,2,0:T(1,128)}, u32[]{:S(2)}) %copy-start) | copy-done | bytes 40
  1.3 46.4 %shampoo_step.1 = (bf16[2,32,256]{2,1,0:T(8,128)(2,1)S(1)}, f32[2,256,256]{2,1,0:T(8,128)S(1)}) custom-call(bf16[4,12,2,4,16,256]{5,4,3,2,1,0:T(8,128)(2,1)} %bitcast.5, f32[2,256,256]{2,1,0:T(8,128)} %bitcast.6, s32[4]{0:T(128)S(1)} %bitcast.4), custom_call_target="tpu_custom_call" | custom-call | tf_op jit(solution)/shard_map/shampoo_step/pallas_call | solution.py:417
  47.7 0.8 %write_out.1 = (bf16[2,32,256]{2,1,0:T(8,128)(2,1)}, f32[2,256,256]{2,1,0:T(8,128)}) custom-call(bf16[2,32,256]{2,1,0:T(8,128)(2,1)S(1)} %get-tuple-element.6.update_in, f32[2,256,256]{2,1,0:T(8,128)S(1)} %get-tuple-element.7.stats_in), custom_call_target="tpu_custom_call" | custom-call | tf_op jit(solution)/shard_map/write_out/pallas_call | solution.py:470
Async XLA Ops:
  0.6 0.7 %copy-start = (s32[1,4,1]{1,2,0:T(1,128)S(1)}, s32[1,4,1]{1,2,0:T(1,128)}, u32[]{:S(2)}) copy-start(s32[1,4,1]{1,2,0:T(1,128)} %param.5) | copy-start | bytes 52
